TPU v7x, 32 devices: a whole 2x2x4 slice. The times are simulated.
32 devices in a mesh: row: 4 (over z), col: 8 (over y, x, core).
Axes of the slice: x: 2, y: 2, z: 4, core: 2. Of those that a mesh axis runs over, the one named last changes fastest.
Arguments:
- velocity: float32 [2, 512, 64, 384], P(None, 'col', 'row'), may hold values from -6 to 6
- synthesis: float32 [384, 384], replicated
- analysis: float32 [384, 384], replicated
- radial_eigen: float32 [384], replicated, may hold values from 0.05 to 4
- pair_list: int32 [64, 2], replicated, may hold values from 0 to 511, as said below
- owner_slot: int32 [64], replicated, may hold values from 0 to 63, each once
- freq_list: int32 [4], replicated, may hold values from 0 to 255
- snap_index: int32 [1], replicated, may hold values from 0 to 254
- block_dft: float32 [64, 4, 2, 384], P(('row', 'col')), may hold values from -6 to 6
- spectra: float32 [64, 4, 2, 384, 384], P(('row', 'col')), may hold values from -6 to 6
Outputs:
- velocity_next: float32 [2, 512, 64, 384], P(None, 'col', 'row')
- block_sums: float32 [64, 4, 2, 384], P(('row', 'col'))
- spectra_next: float32 [64, 4, 2, 384, 384], P(('row', 'col'))
Inputs may be any that keep to these rules, and one draw needn't show every extreme that they name: `pair_list`: the pairs are distinct; the axial index is below 64 and the wavenumber below 512. Of the devices of the solver layout (row index times the size of col plus col index, holding axial indices row * 16 onward and wavenumbers col * 512 / size of col onward), each holds at most 8 selected pairs and some hold exactly 8. `owner_slot`: each slot once.
All inputs are finite; a program needn't handle non-finite values.
Results may differ from a plain program's by a relative error of at most 0.0001.
Values sent between devices are 32-bit elements; how exact they have to be, the bound alone decides.
A program may use at most 128 MiB of HBM per device.

v0:
```python
import math

import numpy as np

import jax
import jax.numpy as jnp
import ml_dtypes
from jax import lax
from jax.experimental import pallas as pl
from jax.experimental.pallas import tpu as pltpu
from jax.sharding import PartitionSpec as P

NBLK = 256


viscosity = 4e-06
axial_scale = 2.0
nonlinear_gain = 0.1
highest = lax.Precision.HIGHEST


def quarter_tables(mode_count):
    points = 3 * mode_count
    quarter = points // 4
    mode_ids = np.arange(mode_count).reshape(-1, 2).T
    point_ids = 2 * np.arange(quarter) + 1
    angle = (point_ids[None, :, None] * mode_ids[:, None, :] % (2 * points)) * (math.pi / points)
    weight = np.where(mode_ids == 0, 1.0, 2.0)[:, None, :] * mode_count**-0.5
    keeping = np.where(mode_ids == 0, 0.0, 4.0 * math.sqrt(mode_count) / points)[:, None, :]
    both = np.stack([np.cos(angle), -np.sin(angle)])
    return both * weight, np.swapaxes(both * keeping, 2, 3)


def halves(table):
    upper = table.astype(ml_dtypes.bfloat16)
    lower = (table - upper.astype(np.float64)).astype(ml_dtypes.bfloat16)
    return np.stack([upper, lower])


def split_two(value):
    upper = value.astype(jnp.bfloat16)
    return upper, (value - upper.astype(jnp.float32)).astype(jnp.bfloat16)


def dot(left, right):
    return jnp.dot(left, right, preferred_element_type=jnp.float32)


def dot_three(left, right):
    return dot(left[0], right[0]) + (dot(left[0], right[1]) + dot(left[1], right[0]))


def steps_kernel(
    field_ref, synth_ref, anal_ref, analysis_ref, synthesis_ref, damping_ref, pick_ref, out_ref, snaps_ref
):
    owners, _, _, _, each, radial_pts = field_ref.shape
    half = owners * each

    @pl.when(pl.program_id(0) == 0)
    def _():
        snaps_ref[...] = jnp.zeros_like(snaps_ref)

    out_ref[...] = field_ref[...]

    def step(section_index, carry):
        parts = []
        for c in range(2):
            for p in range(2):
                now = split_two(out_ref[:, 0, c, p].reshape(half, radial_pts))
                parts.append(dot_three((synth_ref[0, c, p], synth_ref[1, c, p]), now))
        ce, co, se, so = parts
        pairs = (
            (ce * ce + co * co + se * se + so * so, 2.0 * (ce * co + se * so)),
            (2.0 * (ce * se + co * so), 2.0 * (ce * so + co * se)),
        )
        to_eigen = split_two(analysis_ref[...])
        to_points = split_two(synthesis_ref[...])
        for c in range(2):
            snap = jnp.zeros(snaps_ref.shape[2:], jnp.float32)
            for p in range(2):
                forcing = dot_three((anal_ref[0, c, p], anal_ref[1, c, p]), split_two(pairs[c][p]))
                rhs = out_ref[:, 0, c, p].reshape(half, radial_pts) - nonlinear_gain * forcing
                coeffs = dot_three(split_two(rhs), to_eigen) * damping_ref[0, p]
                after = dot_three(split_two(coeffs), to_points)
                out_ref[:, 0, c, p] = after.reshape(owners, each, radial_pts)
                upper, lower = split_two(after)
                snap += dot(pick_ref[0, p], upper) + dot(pick_ref[0, p], lower)
            snaps_ref[section_index, c] += snap
        return carry

    lax.fori_loop(0, 2, step, 0)


def run_steps(field, synth, anal, analysis, synthesis, damping, pick):
    owners, share, _, _, each, radial_pts = field.shape
    selected = pick.shape[2]

    def whole(array):
        return pl.BlockSpec(array.shape, lambda k: (0,) * array.ndim)

    def one(array):
        return pl.BlockSpec((1, *array.shape[1:]), lambda k: (k,) + (0,) * (array.ndim - 1))

    field_spec = pl.BlockSpec((owners, 1, 2, 2, each, radial_pts), lambda k: (0, k, 0, 0, 0, 0))
    return pl.pallas_call(
        steps_kernel,
        grid=(share,),
        in_specs=[
            field_spec, whole(synth), whole(anal), whole(analysis), whole(synthesis), one(damping), one(pick)
        ],
        out_specs=[field_spec, pl.BlockSpec((2, 2, selected, radial_pts), lambda k: (0, 0, 0, 0))],
        out_shape=[
            jax.ShapeDtypeStruct(field.shape, jnp.float32),
            jax.ShapeDtypeStruct((2, 2, selected, radial_pts), jnp.float32),
        ],
        compiler_params=pltpu.CompilerParams(vmem_limit_bytes=50 * 2**20),
    )(field, synth, anal, analysis, synthesis, damping, pick)


def window_terms(freq_list, snap_now):
    position = snap_now.astype(jnp.float32)
    window = 0.54 - 0.46 * jnp.cos(2.0 * math.pi * position / NBLK)
    phase = (freq_list * snap_now % NBLK).astype(jnp.float32) * (2.0 * math.pi / NBLK)
    return (window * jnp.cos(phase), -window * jnp.sin(phase))


def add_snapshot(block, snapshot, real_w, imag_w):
    real_new = (
        block[:, :, 0]
        + real_w[None, :, None] * snapshot[0][:, None, :]
        - imag_w[None, :, None] * snapshot[1][:, None, :]
    )
    imag_new = (
        block[:, :, 1]
        + real_w[None, :, None] * snapshot[1][:, None, :]
        + imag_w[None, :, None] * snapshot[0][:, None, :]
    )
    return jnp.stack([real_new, imag_new], axis=2)


def spectral_update(spectrum_one, old_block, new_block):
    old_real, old_imag = (old_block[:, 0], old_block[:, 1])
    new_real, new_imag = (new_block[:, 0], new_block[:, 1])
    left_real = jnp.stack([new_real, new_imag, old_real, old_imag], axis=1)
    left_imag = jnp.stack([new_imag, -new_real, old_imag, -old_real], axis=1)
    left = jnp.stack([left_real, left_imag], axis=1)
    right = jnp.stack([new_real, new_imag, -old_real, -old_imag], axis=1)
    return spectrum_one + jnp.einsum("fckr,fkq->fcrq", left, right, precision=highest)


def local(
    velocity,
    synthesis,
    analysis,
    radial_eigen,
    pair_list,
    owner_slot,
    freq_list,
    snap_index,
    block_dft,
    spectra,
):
    modes_dev = velocity.shape[1]
    axial_dev = velocity.shape[2]
    col_count = lax.axis_size("col")
    modes_all = modes_dev * col_count
    synth, anal = quarter_tables(modes_all)
    synth, anal = jnp.asarray(halves(synth)), jnp.asarray(halves(anal))
    row_index = lax.axis_index("row")
    col_index = lax.axis_index("col")
    row_count = lax.axis_size("row")
    share = axial_dev // col_count
    base = row_index * axial_dev + col_index * share
    selected = pair_list.shape[0]
    slot_ids = jnp.arange(selected, dtype=jnp.int32)
    of_slot = (owner_slot[None, :] == slot_ids[:, None]).astype(jnp.int32)
    chosen = jnp.sum(of_slot[:, :, None] * pair_list[None], axis=1)
    axial_sel, mode_sel = (chosen[:, 0] - base, chosen[:, 1])
    mode_ids = jnp.asarray(np.arange(modes_all, dtype=np.int32).reshape(-1, 2).T)
    hit_axial = axial_sel[None, :] == jnp.arange(share, dtype=jnp.int32)[:, None]
    hit_mode = mode_sel[None, :, None] == mode_ids[:, None, :]
    pick = (hit_axial[:, None, :, None] & hit_mode[None]).astype(jnp.bfloat16)
    axial_ids = (base + jnp.arange(share, dtype=jnp.int32)).astype(jnp.float32) * axial_scale
    damping = 1.0 / (
        1.0
        + viscosity
        * (axial_ids[:, None, None, None] ** 2 + mode_ids.astype(jnp.float32)[None, :, :, None] ** 2)
        + radial_eigen
    )
    radial_pts = velocity.shape[3]
    each = modes_dev // 2
    outgoing = velocity.reshape(2, each, 2, axial_dev, radial_pts).transpose(3, 0, 2, 1, 4)
    field = lax.all_to_all(
        outgoing.reshape(col_count, share, 2, 2, each, radial_pts), "col", split_axis=0, concat_axis=0, tiled=True
    )
    state, snaps = run_steps(field, synth, anal, analysis, synthesis, damping, pick)
    dense = snaps.reshape(2, 2, row_count, col_count, -1, radial_pts)
    part = jnp.sum(lax.all_to_all(dense, "col", split_axis=3, concat_axis=3, tiled=True), axis=3)
    mine = jnp.sum(lax.all_to_all(part, "row", split_axis=2, concat_axis=2, tiled=True), axis=2)
    back = lax.all_to_all(state, "col", split_axis=0, concat_axis=0, tiled=True)
    back = back.reshape(axial_dev, 2, 2, each, radial_pts).transpose(1, 3, 2, 0, 4)
    current = back.reshape(velocity.shape)
    block = block_dft
    for section_index in range(2):
        real_w, imag_w = window_terms(freq_list, snap_index[0] + section_index)
        block = add_snapshot(block, mine[section_index], real_w, imag_w)
    spectra_next = jax.vmap(spectral_update)(spectra, block_dft, block)
    return (current, block, spectra_next)


def solution(mesh):
    return jax.shard_map(
        local,
        mesh=mesh,
        in_specs=(
            P(None, "col", "row", None),
            P(),
            P(),
            P(),
            P(),
            P(),
            P(),
            P(),
            P(("row", "col"), None, None, None),
            P(("row", "col"), None, None, None, None),
        ),
        out_specs=(
            P(None, "col", "row", None),
            P(("row", "col"), None, None, None),
            P(("row", "col"), None, None, None, None),
        ),
        check_vma=False,
    )
```

profile of v0, /device:TPU:0, one launch (start us, length us, event | category | flops | bytes accessed | tf_op | source)
XLA Modules:
  0.0 154.0 jit_solution(17425251216070231235)
XLA Ops:
  0.6 5.4 %copy.36 = f32[2,32,2,16,384]{4,1,2,0,3:T(8,128)} copy(f32[2,32,2,16,384]{4,3,2,1,0:T(8,128)} %bitcast.34) | data formatting | bytes 6291456 | tf_op jit(solution)/shard_map/reshape | solution.py:192
  6.0 0.0 copy-start
  6.0 0.0 copy-start.1
  6.1 5.4 %all-to-all-start = ((f32[8,2,2,2,32,384]{5,4,3,2,1,0:T(8,128)}), f32[8,2,2,2,32,384]{5,4,3,2,1,0:T(8,128)}, u32[]{:S(2)}, u32[]{:S(2)}) async-start(f32[8,2,2,2,32,384]{5,4,3,2,1,0:T(8,128)} %bitcast.33), calls=%async_computation | async-start | bytes 6291456 | tf_op jit(solution)/shard_map/all_to_all | solution.py:193
  11.6 0.1 multiply_reduce_fusion
  11.7 0.1 multiply_add_fusion.1
  11.8 0.1 broadcast_compare_fusion
  11.9 0.1 and_convert_fusion.pick_ref
  12.0 1.4 add_divide_fusion.damping_ref
  13.4 36.1 %all-to-all-done.field_ref = f32[8,2,2,2,32,384]{5,4,3,2,1,0:T(8,128)} async-done(((f32[8,2,2,2,32,384]{5,4,3,2,1,0:T(8,128)}), f32[8,2,2,2,32,384]{5,4,3,2,1,0:T(8,128)}, u32[]{:S(2)}, u32[]{:S(2)}) %all-to-all-start) | async-done | bytes 3145760 | tf_op jit(solution)/shard_map/all_to_all | solution.py:193
  49.5 37.1 %shard_map.148 = (f32[8,2,2,2,32,384]{5,4,3,2,1,0:T(8,128)}, f32[2,2,64,384]{3,2,1,0:T(8,128)S(1)}) custom-call(f32[8,2,2,2,32,384]{5,4,3,2,1,0:T(8,128)} %all-to-all-done.field_ref, bf16[2,2,2,384,256]{4,3,2,1,0:T(8,128)(2,1)S(1)} %copy-done, bf16[2,2,2,256,384]{4,3,2,1,0:T(8,128)(2,1)} %constant.63.clone.anal_ref, f32[384,384]{1,0:T(8,128)S(1)} %copy-done.1, ...), custom_call_target="tpu_custom_call" | custom-call | tf_op jit(solution)/shard_map/pallas_call | solution.py:105
  86.6 0.2 reshape.134
  86.9 0.1 copy.39
  87.0 10.7 %all_to_all.20 = f32[2,2,4,8,2,384]{5,4,2,1,0,3:T(2,128)S(1)} all-to-all(f32[2,2,4,8,2,384]{5,4,2,1,0,3:T(2,128)S(1)} %copy.39), channel_id=1, replica_groups=mesh['row'=4,'col'=8] {'col'}, dimensions={3} | all-to-all | bytes 786432 | tf_op jit(solution)/shard_map/all_to_all | solution.py:198
  97.7 0.1 reduce_sum.28
  97.9 11.1 %all_to_all.21 = f32[2,2,4,2,384]{4,3,1,0,2:T(2,128)S(1)} all-to-all(f32[2,2,4,2,384]{4,3,1,0,2:T(2,128)S(1)} %copy.40), channel_id=1, replica_groups=mesh['row'=4,'col'=8] {'row'}, dimensions={2} | all-to-all | bytes 98304 | tf_op jit(solution)/shard_map/all_to_all | solution.py:199
  108.9 4.0 %all-to-all-start.1 = ((f32[8,2,2,2,32,384]{5,4,3,2,1,0:T(8,128)}), f32[8,2,2,2,32,384]{5,4,3,2,1,0:T(8,128)S(1)}, u32[]{:S(2)}, u32[]{:S(2)}) async-start(f32[8,2,2,2,32,384]{5,4,3,2,1,0:T(8,128)} %get-tuple-element.5), calls=%async_computation.1 | async-start | bytes 6291456 | tf_op jit(solution)/shard_map/all_to_all | solution.py:200
  113.7 0.1 cosine_multiply_fusion.1
  113.8 0.1 sine_multiply_fusion
  113.9 0.1 slice_negate_fusion.1
  114.0 0.6 copy.45
  114.7 13.9 %convolution_add_fusion = f32[2,4,2,384,384]{4,3,2,1,0:T(8,128)} fusion(f32[2,4,2,384,384]{4,3,2,1,0:T(8,128)} %param.22, f32[2,4,2,4,384]{4,1,3,0,2:T(4,128)S(1)} %pad_maximum_fusion, f32[2,4,4,384,1]{3,1,2,0,4:T(4,128)S(1)} %get-tuple-element.17), kind=kOutput, calls=%fused_computation | convolution fusion | flops 115605504 | bytes 19021824 | tf_op jit(solution)/shard_map/vmap(fckr,fkq->fcrq)/dot_general | solution.py:148
  128.6 21.9 %all-to-all-done.1 = f32[8,2,2,2,32,384]{5,4,3,2,1,0:T(8,128)S(1)} async-done(((f32[8,2,2,2,32,384]{5,4,3,2,1,0:T(8,128)}), f32[8,2,2,2,32,384]{5,4,3,2,1,0:T(8,128)S(1)}, u32[]{:S(2)}, u32[]{:S(2)}) %all-to-all-start.1) | async-done | bytes 3145760 | tf_op jit(solution)/shard_map/all_to_all | solution.py:200
  150.5 3.5 %copy.37 = f32[2,32,2,16,384]{4,3,2,1,0:T(8,128)} copy(f32[2,32,2,16,384]{4,1,2,0,3:T(8,128)S(1)} %bitcast.32) | data formatting | bytes 6291456 | tf_op jit(solution)/shard_map/transpose | solution.py:201
  (29 shorter events, 0.2 us)
Async XLA Ops:
  6.0 5.5 %copy-start.8 = (s32[64]{0:T(128)S(1)}, s32[64]{0:T(128)}, u32[]{:S(2)}) copy-start(s32[64]{0:T(128)} %param.18) | copy-start | bytes 772
  6.0 5.5 %copy-start.7 = (s32[64,2]{0,1:T(2,128)S(1)}, s32[64,2]{0,1:T(2,128)}, u32[]{:S(2)}) copy-start(s32[64,2]{0,1:T(2,128)} %param.17) | copy-start | bytes 1540
  6.0 5.7 %copy-start.6 = (f32[2,256]{1,0:T(2,128)S(1)}, f32[2,256]{1,0:T(2,128)}, u32[]{:S(2)}) copy-start(f32[2,256]{1,0:T(2,128)} %constant.68) | copy-start | bytes 6148
  6.0 5.8 %copy-start.5 = (s32[2,256]{1,0:T(2,128)S(1)}, s32[2,256]{1,0:T(2,128)}, u32[]{:S(2)}) copy-start(s32[2,256]{1,0:T(2,128)} %constant.64.clone) | copy-start | bytes 6148
  6.0 6.0 %copy-start.4 = (f32[384]{0:T(512)S(1)}, f32[384]{0:T(512)}, u32[]{:S(2)}) copy-start(f32[384]{0:T(512)} %param.16) | copy-start | bytes 4612
  6.0 43.5 %copy-start = (bf16[2,2,2,384,256]{4,3,2,1,0:T(8,128)(2,1)S(1)}, bf16[2,2,2,384,256]{4,3,2,1,0:T(8,128)(2,1)}, u32[]{:S(2)}) copy-start(bf16[2,2,2,384,256]{4,3,2,1,0:T(8,128)(2,1)} %constant.62.clone.synth_ref) | copy-start | bytes 4718596
  6.0 43.5 %copy-start.1 = (f32[384,384]{1,0:T(8,128)S(1)}, f32[384,384]{1,0:T(8,128)}, u32[]{:S(2)}) copy-start(f32[384,384]{1,0:T(8,128)} %analysis_ref.1) | copy-start | bytes 1769476
  6.1 43.5 %copy-start.2 = (f32[384,384]{1,0:T(8,128)S(1)}, f32[384,384]{1,0:T(8,128)}, u32[]{:S(2)}) copy-start(f32[384,384]{1,0:T(8,128)} %synthesis_ref.1) | copy-start | bytes 1769476
  6.1 43.4 %all-to-all-start = ((f32[8,2,2,2,32,384]{5,4,3,2,1,0:T(8,128)}), f32[8,2,2,2,32,384]{5,4,3,2,1,0:T(8,128)}, u32[]{:S(2)}, u32[]{:S(2)}) async-start(f32[8,2,2,2,32,384]{5,4,3,2,1,0:T(8,128)} %bitcast.33), calls=%async_computation | async-start | bytes 6291456 | tf_op jit(solution)/shard_map/all_to_all | solution.py:193
  108.9 4.8 %copy-start.3 = (f32[2,4,2,384]{3,2,1,0:T(2,128)S(1)}, f32[2,4,2,384]{3,2,1,0:T(2,128)}, u32[]{:S(2)}) copy-start(f32[2,4,2,384]{3,2,1,0:T(2,128)} %param.21) | copy-start | bytes 73732
  108.9 4.8 %copy-start.9 = (s32[4]{0:T(128)S(1)}, s32[4]{0:T(128)}, u32[]{:S(2)}) copy-start(s32[4]{0:T(128)} %param.19) | copy-start | bytes 52
  108.9 41.6 %all-to-all-start.1 = ((f32[8,2,2,2,32,384]{5,4,3,2,1,0:T(8,128)}), f32[8,2,2,2,32,384]{5,4,3,2,1,0:T(8,128)S(1)}, u32[]{:S(2)}, u32[]{:S(2)}) async-start(f32[8,2,2,2,32,384]{5,4,3,2,1,0:T(8,128)} %get-tuple-element.5), calls=%async_computation.1 | async-start | bytes 6291456 | tf_op jit(solution)/shard_map/all_to_all | solution.py:200
where the time goes:
time: 154 us
  waiting for transfers between devices  58 us (38%)
  Pallas kernels  37.1 us (24%)
  blocking collectives  21.8 us (14%)
  matrix products  13.9 us (9%)
  local copies, waits for them, and re-layouts  9.89 us (6%)
  starting transfers between devices  9.41 us (6%)
  other arithmetic  2.23 us (1%)
  between operations  1.66 us (1%)
    pallas_call x1, Pallas kernels, run_steps(): pl.pallas_call(steps_kernel, grid=(share,), in_specs=[field_spec, whole(s...  37.1 us
    all_to_all x1, waiting for transfers between devices, local(): lax.all_to_all(outgoing.reshape(col_count, share, 2, 2, each, radial_pts)...  36.1 us
    all_to_all x1, waiting for transfers between devices, local(): back = lax.all_to_all(state, 'col', split_axis=0, concat_axis=0, tiled=True)  21.9 us
    dot_general x1, matrix products, spectral_update(): jnp.einsum('fckr,fkq->fcrq', left, right, precision=highest)  13.9 us
    all_to_all x1, blocking collectives, local(): lax.all_to_all(part, 'row', split_axis=2, concat_axis=2, tiled=True)  11.1 us
    all_to_all x1, blocking collectives, local(): lax.all_to_all(dense, 'col', split_axis=3, concat_axis=3, tiled=True)  10.7 us
    all_to_all x1, starting transfers between devices, local(): lax.all_to_all(outgoing.reshape(col_count, share, 2, 2, each, radial_pts)...  5.45 us
    reshape x1, local copies, waits for them, and re-layouts, local(): velocity.reshape(2, each, 2, axial_dev, radial_pts).transpose(3, 0, 2, 1, 4)  5.38 us
  transfers between devices with their start and end apart: 2, of which 2 were waited for; matrix products, arithmetic and copies ran while one was open for 11% of the time, Pallas kernels for 0%

commit v1 on v0

--- a/solution.py
+++ b/solution.py
@@ -113,6 +113,9 @@
             jax.ShapeDtypeStruct(field.shape, jnp.float32),
             jax.ShapeDtypeStruct((2, 2, selected, radial_pts), jnp.float32),
         ],
+        cost_estimate=pl.CostEstimate(
+            flops=share * 14 * 10**9, bytes_accessed=share * 8 * 10**6, transcendentals=0
+        ),
         compiler_params=pltpu.CompilerParams(vmem_limit_bytes=50 * 2**20),
     )(field, synth, anal, analysis, synthesis, damping, pick)
 
@@ -190,14 +193,22 @@
     radial_pts = velocity.shape[3]
     each = modes_dev // 2
     outgoing = velocity.reshape(2, each, 2, axial_dev, radial_pts).transpose(3, 0, 2, 1, 4)
-    field = lax.all_to_all(
-        outgoing.reshape(col_count, share, 2, 2, each, radial_pts), "col", split_axis=0, concat_axis=0, tiled=True
-    )
-    state, snaps = run_steps(field, synth, anal, analysis, synthesis, damping, pick)
+    outgoing = outgoing.reshape(col_count, share, 2, 2, each, radial_pts)
+    fields = [
+        lax.all_to_all(outgoing[:, k : k + 1], "col", split_axis=0, concat_axis=0, tiled=True)
+        for k in range(share)
+    ]
+    done = [
+        run_steps(fields[k], synth, anal, analysis, synthesis, damping[k : k + 1], pick[k : k + 1])
+        for k in range(share)
+    ]
+    snaps = sum(snap for _, snap in done)
     dense = snaps.reshape(2, 2, row_count, col_count, -1, radial_pts)
     part = jnp.sum(lax.all_to_all(dense, "col", split_axis=3, concat_axis=3, tiled=True), axis=3)
     mine = jnp.sum(lax.all_to_all(part, "row", split_axis=2, concat_axis=2, tiled=True), axis=2)
-    back = lax.all_to_all(state, "col", split_axis=0, concat_axis=0, tiled=True)
+    back = jnp.concatenate(
+        [lax.all_to_all(state, "col", split_axis=0, concat_axis=0, tiled=True) for state, _ in done], axis=1
+    )
     back = back.reshape(axial_dev, 2, 2, each, radial_pts).transpose(1, 3, 2, 0, 4)
     current = back.reshape(velocity.shape)
     block = block_dft

time: 154 us -> 155 us (level)
  waiting for transfers between devices: 58 us -> 47 us
  starting transfers between devices: 9.41 us -> 17.3 us
  Pallas kernels: 37.1 us -> 40.7 us
    all_to_all x2 -> x4, waiting for transfers between devices: 58 us -> 47 us  [the longest x2 26 us: local(): lax.all_to_all(state, 'col', split_axis=0, concat_axis=0, tiled=True)]
    all_to_all x2 -> x4, starting transfers between devices: 9.41 us -> 17.3 us  [the longest x2 9.75 us: local(): lax.all_to_all(outgoing[:, k:k + 1], 'col', split_axis=0, concat_axis=0,...]
    pallas_call x1 -> x2, Pallas kernels: 37.1 us -> 40.7 us  [run_steps(): pl.pallas_call(steps_kernel, grid=(share,), in_specs=[field_spec, whole(s...]
    slice x0 -> x3, local copies, waits for them, and re-layouts: none -> 1.98 us  [the longest x1 1.87 us: local(): outgoing[:, k:k + 1]]
    reshape x1, local copies, waits for them, and re-layouts: 5.38 us -> 3.71 us  [local(): velocity.reshape(2, each, 2, axial_dev, radial_pts).transpose(3, 0, 2, 1, 4)]
  transfers between devices with their start and end apart: 2 -> 4, of which waited for: 2 -> 4; matrix products, arithmetic and copies ran while one was open for 11% -> 10% of each run, Pallas kernels for 0% -> 13%
where the time goes in v1:
time: 155 us; the launch traced here: 154 us
  waiting for transfers between devices  47 us (30%)
  Pallas kernels  40.7 us (26%)
  blocking collectives  22.3 us (14%)
  starting transfers between devices  17.3 us (11%)
  matrix products  13.9 us (9%)
  local copies, waits for them, and re-layouts  10.2 us (7%)
  between operations  1.71 us (1%)
    pallas_call x2, Pallas kernels, run_steps(): pl.pallas_call(steps_kernel, grid=(share,), in_specs=[field_spec, whole(s...  40.7 us
    all_to_all x2, waiting for transfers between devices, local(): lax.all_to_all(state, 'col', split_axis=0, concat_axis=0, tiled=True)  26 us
    all_to_all x2, waiting for transfers between devices, local(): lax.all_to_all(outgoing[:, k:k + 1], 'col', split_axis=0, concat_axis=0,...  21 us
    dot_general x1, matrix products, spectral_update(): jnp.einsum('fckr,fkq->fcrq', left, right, precision=highest)  13.9 us
    all_to_all x1, blocking collectives, local(): lax.all_to_all(dense, 'col', split_axis=3, concat_axis=3, tiled=True)  11.4 us
    all_to_all x1, blocking collectives, local(): lax.all_to_all(part, 'row', split_axis=2, concat_axis=2, tiled=True)  10.8 us
    all_to_all x2, starting transfers between devices, local(): lax.all_to_all(outgoing[:, k:k + 1], 'col', split_axis=0, concat_axis=0,...  9.75 us
    all_to_all x2, starting transfers between devices, local(): lax.all_to_all(state, 'col', split_axis=0, concat_axis=0, tiled=True)  7.51 us
  transfers between devices with their start and end apart: 4, of which 4 were waited for; matrix products, arithmetic and copies ran while one was open for 10% of the time, Pallas kernels for 13%

profile of v1, /device:TPU:0, one launch (start us, length us, event | category | flops | bytes accessed | tf_op | source)
XLA Modules:
  0.0 154.3 jit_solution(17435012062585634784)
XLA Ops:
  0.6 3.7 %copy.36 = f32[2,32,2,16,384]{4,1,2,0,3:T(8,128)S(1)} copy(f32[2,32,2,16,384]{4,3,2,1,0:T(8,128)} %bitcast.34) | data formatting | bytes 6291456 | tf_op jit(solution)/shard_map/reshape | solution.py:195
  4.3 1.9 %fusion.12 = (f32[8,1,2,2,32,384]{5,4,3,2,1,0:T(8,128)}, f32[8,1,2,2,32,384]{5,4,3,2,1,0:T(8,128)}) fusion(f32[8,2,2,2,32,384]{5,4,3,2,1,0:T(8,128)S(1)} %bitcast.32), kind=kLoop, calls=%fused_computation.46 | loop fusion | bytes 6291456 | tf_op jit(solution)/shard_map/slice | solution.py:198
  6.2 5.3 %all-to-all-start = ((f32[8,1,2,2,32,384]{5,4,3,2,1,0:T(8,128)}), f32[8,1,2,2,32,384]{5,4,3,2,1,0:T(8,128)}, u32[]{:S(2)}, u32[]{:S(2)}) async-start(f32[8,1,2,2,32,384]{5,4,3,2,1,0:T(8,128)} %get-tuple-element.20), calls=%async_computation | async-start | bytes 3145728 | tf_op jit(solution)/shard_map/all_to_all | solution.py:198
  11.6 0.1 multiply_reduce_fusion
  12.0 0.3 add_divide_fusion
  12.3 0.1 fusion.13
  12.4 20.3 %all-to-all-done.field_ref = f32[8,1,2,2,32,384]{5,4,3,2,1,0:T(8,128)} async-done(((f32[8,1,2,2,32,384]{5,4,3,2,1,0:T(8,128)}), f32[8,1,2,2,32,384]{5,4,3,2,1,0:T(8,128)}, u32[]{:S(2)}, u32[]{:S(2)}) %all-to-all-start) | async-done | bytes 1572896 | tf_op jit(solution)/shard_map/all_to_all | solution.py:198
  32.7 4.4 %all-to-all-start.2 = ((f32[8,1,2,2,32,384]{5,4,3,2,1,0:T(8,128)}), f32[8,1,2,2,32,384]{5,4,3,2,1,0:T(8,128)}, u32[]{:S(2)}, u32[]{:S(2)}) async-start(f32[8,1,2,2,32,384]{5,4,3,2,1,0:T(8,128)} %get-tuple-element.21), calls=%async_computation.2 | async-start | bytes 3145728 | tf_op jit(solution)/shard_map/all_to_all | solution.py:198
  37.2 20.3 %shard_map.148 = (f32[8,1,2,2,32,384]{5,4,3,2,1,0:T(8,128)}, f32[2,2,64,384]{3,2,1,0:T(8,128)S(1)}) custom-call(f32[8,1,2,2,32,384]{5,4,3,2,1,0:T(8,128)} %all-to-all-done.field_ref, bf16[2,2,2,384,256]{4,3,2,1,0:T(8,128)(2,1)} %constant.62.clone.synth_ref, bf16[2,2,2,256,384]{4,3,2,1,0:T(8,128)(2,1)} %constant.63.clone.anal_ref, f32[384,384]{1,0:T(8,128)S(1)} %copy-done, ...), custom_call_target="tpu_custom_call" | custom-call | flops 14000000000 | bytes 8000000 | tf_op jit(solution)/shard_map/pallas_call | solution.py:105
  57.4 0.7 all-to-all-done.2.field_ref
  58.2 20.4 %shard_map.149 = (f32[8,1,2,2,32,384]{5,4,3,2,1,0:T(8,128)}, f32[2,2,64,384]{3,2,1,0:T(8,128)S(1)}) custom-call(f32[8,1,2,2,32,384]{5,4,3,2,1,0:T(8,128)} %all-to-all-done.2.field_ref, bf16[2,2,2,384,256]{4,3,2,1,0:T(8,128)(2,1)} %constant.62.clone.synth_ref, bf16[2,2,2,256,384]{4,3,2,1,0:T(8,128)(2,1)} %constant.63.clone.anal_ref, f32[384,384]{1,0:T(8,128)S(1)} %copy-done, ...), custom_call_target="tpu_custom_call" | custom-call | flops 14000000000 | bytes 8000000 | tf_op jit(solution)/shard_map/pallas_call | solution.py:105
  78.6 0.2 reshape.134
  78.9 0.1 copy.39
  79.0 11.4 %all_to_all.30 = f32[2,2,4,8,2,384]{5,4,2,1,0,3:T(2,128)S(1)} all-to-all(f32[2,2,4,8,2,384]{5,4,2,1,0,3:T(2,128)S(1)} %copy.39), channel_id=1, replica_groups=mesh['row'=4,'col'=8] {'col'}, dimensions={3} | all-to-all | bytes 786432 | tf_op jit(solution)/shard_map/all_to_all | solution.py:207
  90.4 0.1 reduce_sum.28
  90.6 10.8 %all_to_all.31 = f32[2,2,4,2,384]{4,3,1,0,2:T(2,128)S(1)} all-to-all(f32[2,2,4,2,384]{4,3,1,0,2:T(2,128)S(1)} %copy.40), channel_id=1, replica_groups=mesh['row'=4,'col'=8] {'row'}, dimensions={2} | all-to-all | bytes 98304 | tf_op jit(solution)/shard_map/all_to_all | solution.py:208
  101.4 3.7 %all-to-all-start.1 = ((f32[8,1,2,2,32,384]{5,4,3,2,1,0:T(8,128)}), f32[8,1,2,2,32,384]{5,4,3,2,1,0:T(8,128)S(1)}, u32[]{:S(2)}, u32[]{:S(2)}) async-start(f32[8,1,2,2,32,384]{5,4,3,2,1,0:T(8,128)} %get-tuple-element.7), calls=%async_computation.1 | async-start | bytes 3145728 | tf_op jit(solution)/shard_map/all_to_all | solution.py:210
  106.1 20.0 %all-to-all-done.1 = f32[8,1,2,2,32,384]{5,4,3,2,1,0:T(8,128)S(1)} async-done(((f32[8,1,2,2,32,384]{5,4,3,2,1,0:T(8,128)}), f32[8,1,2,2,32,384]{5,4,3,2,1,0:T(8,128)S(1)}, u32[]{:S(2)}, u32[]{:S(2)}) %all-to-all-start.1) | async-done | bytes 1572896 | tf_op jit(solution)/shard_map/all_to_all | solution.py:210
  126.1 3.8 %all-to-all-start.3 = ((f32[8,1,2,2,32,384]{5,4,3,2,1,0:T(8,128)}), f32[8,1,2,2,32,384]{5,4,3,2,1,0:T(8,128)S(1)}, u32[]{:S(2)}, u32[]{:S(2)}) async-start(f32[8,1,2,2,32,384]{5,4,3,2,1,0:T(8,128)} %get-tuple-element.8), calls=%async_computation.3 | async-start | bytes 3145728 | tf_op jit(solution)/shard_map/all_to_all | solution.py:210
  130.0 0.6 copy.45
  130.7 13.9 %convolution_add_fusion = f32[2,4,2,384,384]{4,3,2,1,0:T(8,128)} fusion(f32[2,4,2,384,384]{4,3,2,1,0:T(8,128)} %param.22, f32[2,4,2,4,384]{4,1,3,0,2:T(4,128)S(1)} %pad_maximum_fusion.1, f32[2,4,4,384,1]{3,1,2,0,4:T(4,128)S(1)} %get-tuple-element.27), kind=kOutput, calls=%fused_computation | convolution fusion | flops 115605504 | bytes 19021824 | tf_op jit(solution)/shard_map/vmap(fckr,fkq->fcrq)/dot_general | solution.py:151
  144.6 6.0 %all-to-all-done.3 = f32[8,1,2,2,32,384]{5,4,3,2,1,0:T(8,128)S(1)} async-done(((f32[8,1,2,2,32,384]{5,4,3,2,1,0:T(8,128)}), f32[8,1,2,2,32,384]{5,4,3,2,1,0:T(8,128)S(1)}, u32[]{:S(2)}, u32[]{:S(2)}) %all-to-all-start.3) | async-done | bytes 1572896 | tf_op jit(solution)/shard_map/all_to_all | solution.py:210
  150.6 0.2 pad_maximum_fusion
  150.8 3.5 %copy.37 = f32[2,32,2,16,384]{4,3,2,1,0:T(8,128)} copy(f32[2,32,2,16,384]{4,1,2,0,3:T(8,128)S(1)} %bitcast.33) | data formatting | bytes 6291456 | tf_op jit(solution)/shard_map/transpose | solution.py:212
  (37 shorter events, 0.7 us)
Async XLA Ops:
  6.2 5.3 %copy-start.7 = (s32[64]{0:T(128)S(1)}, s32[64]{0:T(128)}, u32[]{:S(2)}) copy-start(s32[64]{0:T(128)} %param.18) | copy-start | bytes 772
  6.2 5.4 %copy-start.6 = (s32[64,2]{0,1:T(2,128)S(1)}, s32[64,2]{0,1:T(2,128)}, u32[]{:S(2)}) copy-start(s32[64,2]{0,1:T(2,128)} %param.17) | copy-start | bytes 1540
  6.2 5.5 %copy-start.5 = (f32[2,256]{1,0:T(2,128)S(1)}, f32[2,256]{1,0:T(2,128)}, u32[]{:S(2)}) copy-start(f32[2,256]{1,0:T(2,128)} %constant.68) | copy-start | bytes 6148
  6.2 5.6 %copy-start.4 = (s32[2,256]{1,0:T(2,128)S(1)}, s32[2,256]{1,0:T(2,128)}, u32[]{:S(2)}) copy-start(s32[2,256]{1,0:T(2,128)} %constant.64.clone) | copy-start | bytes 6148
  6.2 5.8 %copy-start.3 = (f32[384]{0:T(512)S(1)}, f32[384]{0:T(512)}, u32[]{:S(2)}) copy-start(f32[384]{0:T(512)} %param.16) | copy-start | bytes 4612
  6.2 26.4 %all-to-all-start = ((f32[8,1,2,2,32,384]{5,4,3,2,1,0:T(8,128)}), f32[8,1,2,2,32,384]{5,4,3,2,1,0:T(8,128)}, u32[]{:S(2)}, u32[]{:S(2)}) async-start(f32[8,1,2,2,32,384]{5,4,3,2,1,0:T(8,128)} %get-tuple-element.20), calls=%async_computation | async-start | bytes 3145728 | tf_op jit(solution)/shard_map/all_to_all | solution.py:198
  32.7 4.5 %copy-start = (f32[384,384]{1,0:T(8,128)S(1)}, f32[384,384]{1,0:T(8,128)}, u32[]{:S(2)}) copy-start(f32[384,384]{1,0:T(8,128)} %analysis_ref.3) | copy-start | bytes 1769476
  32.7 4.5 %copy-start.1 = (f32[384,384]{1,0:T(8,128)S(1)}, f32[384,384]{1,0:T(8,128)}, u32[]{:S(2)}) copy-start(f32[384,384]{1,0:T(8,128)} %synthesis_ref.3) | copy-start | bytes 1769476
  32.7 25.5 %all-to-all-start.2 = ((f32[8,1,2,2,32,384]{5,4,3,2,1,0:T(8,128)}), f32[8,1,2,2,32,384]{5,4,3,2,1,0:T(8,128)}, u32[]{:S(2)}, u32[]{:S(2)}) async-start(f32[8,1,2,2,32,384]{5,4,3,2,1,0:T(8,128)} %get-tuple-element.21), calls=%async_computation.2 | async-start | bytes 3145728 | tf_op jit(solution)/shard_map/all_to_all | solution.py:198
  101.4 4.5 %copy-start.2 = (f32[2,4,2,384]{3,2,1,0:T(2,128)S(1)}, f32[2,4,2,384]{3,2,1,0:T(2,128)}, u32[]{:S(2)}) copy-start(f32[2,4,2,384]{3,2,1,0:T(2,128)} %param.21) | copy-start | bytes 73732
  101.4 4.6 %copy-start.8 = (s32[4]{0:T(128)S(1)}, s32[4]{0:T(128)}, u32[]{:S(2)}) copy-start(s32[4]{0:T(128)} %param.19) | copy-start | bytes 52
  101.4 24.7 %all-to-all-start.1 = ((f32[8,1,2,2,32,384]{5,4,3,2,1,0:T(8,128)}), f32[8,1,2,2,32,384]{5,4,3,2,1,0:T(8,128)S(1)}, u32[]{:S(2)}, u32[]{:S(2)}) async-start(f32[8,1,2,2,32,384]{5,4,3,2,1,0:T(8,128)} %get-tuple-element.7), calls=%async_computation.1 | async-start | bytes 3145728 | tf_op jit(solution)/shard_map/all_to_all | solution.py:210
  126.1 24.5 %all-to-all-start.3 = ((f32[8,1,2,2,32,384]{5,4,3,2,1,0:T(8,128)}), f32[8,1,2,2,32,384]{5,4,3,2,1,0:T(8,128)S(1)}, u32[]{:S(2)}, u32[]{:S(2)}) async-start(f32[8,1,2,2,32,384]{5,4,3,2,1,0:T(8,128)} %get-tuple-element.8), calls=%async_computation.3 | async-start | bytes 3145728 | tf_op jit(solution)/shard_map/all_to_all | solution.py:210
